TPU v7x, 512 devices: a whole 4x4x16 slice. The times are simulated.
512 devices in a mesh: pipe: 2 (over core), dp: 16 (over y, x), tensor: 16 (over z).
Axes of the slice: x: 4, y: 4, z: 16, core: 2. Of those that a mesh axis runs over, the one named last changes fastest.
Arguments:
- x_act: bfloat16 [2, 6144, 16384], P('pipe', 'dp', 'tensor'), may hold values from -6 to 6
- grad_z: bfloat16 [2, 6144, 26624], P('pipe', 'dp', 'tensor'), may hold values from -6 to 6
- weight_tiles: bfloat16 [2, 256, 128, 128], P('pipe', 'tensor'), may hold values from -0.5 to 0.5
- tile_rows: int32 [2, 256], P('pipe', 'tensor'), may hold values from 0 to 127, as said below
- tile_cols: int32 [2, 256], P('pipe', 'tensor'), may hold values from 0 to 12
- err_in: float32 [2, 16, 256, 128, 128], P('pipe', 'dp', 'tensor'), may hold values from -0.3 to 0.3
- kept_mask: int32 [2, 16, 256], P('pipe', 'dp', 'tensor'), may hold values 0 or 1
- tile_list: int32 [2, 16, 192], P('pipe', 'dp', 'tensor'), may hold values from 0 to 23, as said below
- live_count: int32 [2, 16, 16], P('pipe', 'dp', 'tensor'), may hold values from 1 to 12, as said below
Outputs:
- recv_tiles: bfloat16 [2, 16, 192, 128, 128], P('pipe', 'dp', 'tensor')
- err_out: float32 [2, 16, 256, 128, 128], P('pipe', 'dp', 'tensor')
- grad_sum: float32 [2, 16, 16, 128, 128], P('pipe', 'dp', 'tensor')
Inputs may be any that keep to these rules, and one draw needn't show every extreme that they name: `tile_rows`: entry j of a tensor rank's 16 entries of one section names a column block held by tensor rank j // (16 / 16), that is one of the blocks ((j // (16 / 16)) * L to that plus L - 1, L = 16384 / (128 * 16)). `tile_list`: A device's 12 entries are distinct tile numbers m * L + b of its own region (L = 16384 / (128 * 16), m < 3, b < L). `live_count`: some device uses all 12 entries of its list.
All inputs are finite; a program needn't handle non-finite values. No bound on the sum of `kept_mask` on one device may be relied on, other than what follows from the above.
Results may differ from a plain program's by a relative error of at most 0.0048.
Values may be sent and summed in bfloat16 or wider, within the bound.
A program may use at most 128 MiB of HBM per device.

v0:
```python
import jax
import jax.numpy as jnp
from jax import lax
from jax.sharding import PartitionSpec as P


def shifted(value, axis, by):
    count = lax.axis_size(axis)
    return lax.ppermute(value, axis, [(i, (i + by) % count) for i in range(count)])


def pack_listed(input_grad, listed, live_now, tile_size, local_blocks):
    tok_count = input_grad.shape[0]
    grid = input_grad.reshape(tok_count // tile_size, tile_size, local_blocks, tile_size)
    picked = grid[listed // local_blocks, :, listed % local_blocks, :]
    valid = jnp.arange(listed.shape[0], dtype=jnp.int32) < live_now[0]
    return jnp.where(valid[:, None, None], picked, jnp.zeros_like(picked))


def local(
    x_act, grad_z, weight_tiles, tile_rows, tile_cols, err_in, kept_mask, tile_list, live_count
):
    tensor_count = lax.axis_size("tensor")
    inputs = x_act[0]
    grads_out = grad_z[0]
    stored = weight_tiles[0]
    row_ids = tile_rows[0]
    col_ids = tile_cols[0]
    tok_count = inputs.shape[0]
    tile_size = stored.shape[1]
    local_blocks = inputs.shape[1] // tile_size
    local_rows = row_ids % local_blocks
    grad_blocks = grads_out.reshape(tok_count, grads_out.shape[1] // tile_size, tile_size)
    grad_sel = jnp.take(grad_blocks, col_ids, axis=1)
    gathered = lax.all_gather(inputs, "tensor", axis=1, tiled=True)
    input_sel = jnp.take(
        gathered.reshape(tok_count, local_blocks * tensor_count, tile_size), row_ids, axis=1
    )
    weight_grads = jnp.einsum(
        "tkc,tkf->kcf", input_sel, grad_sel, preferred_element_type=jnp.float32
    ) * (1.0 / tok_count)
    accumulated = weight_grads + err_in[0, 0]
    keep_now = (kept_mask[0, 0] == 1)[:, None, None]
    sent_tiles = jnp.where(keep_now, accumulated, jnp.float32(0.0))
    residual = accumulated - sent_tiles
    summed = lax.psum_scatter(sent_tiles, "dp", scatter_dimension=0, tiled=True)
    partial_value = jnp.einsum(
        "tkf,kcf->tkc", grad_sel, stored, preferred_element_type=jnp.float32
    ).astype(jnp.bfloat16)
    arrived_terms, arrived_rows = (
        lax.all_to_all(partial_value, "tensor", split_axis=1, concat_axis=1, tiled=True),
        lax.all_to_all(local_rows[None, :], "tensor", split_axis=1, concat_axis=1, tiled=True),
    )
    onehot = (
        arrived_rows[0][:, None] == jnp.arange(local_blocks, dtype=jnp.int32)[None, :]
    ).astype(jnp.bfloat16)
    input_grad = jnp.einsum(
        "trc,rb->tbc", arrived_terms, onehot, preferred_element_type=jnp.float32
    ).astype(jnp.bfloat16)
    listed = tile_list[0, 0]
    live_now = live_count[0, 0]
    grad_in, listed_in, live_in = shifted((input_grad, listed, live_now), "pipe", -1)
    arrived = pack_listed(grad_in, listed_in, live_in, tile_size, local_blocks)
    return (arrived[None, None], residual[None, None], summed[None, None])


def solution(mesh):
    return jax.shard_map(
        local,
        mesh=mesh,
        in_specs=(
            P("pipe", "dp", "tensor"),
            P("pipe", "dp", "tensor"),
            P("pipe", "tensor", None, None),
            P("pipe", "tensor"),
            P("pipe", "tensor"),
            P("pipe", "dp", "tensor", None, None),
            P("pipe", "dp", "tensor"),
            P("pipe", "dp", "tensor"),
            P("pipe", "dp", "tensor"),
        ),
        out_specs=(
            P("pipe", "dp", "tensor", None, None),
            P("pipe", "dp", "tensor", None, None),
            P("pipe", "dp", "tensor", None, None),
        ),
        check_vma=False,
    )
```

profile of v0, /device:TPU:2, one launch (start us, length us, event | category | flops | bytes accessed | tf_op | source)
XLA Modules:
  0.0 350.0 jit_solution(13440303011730557698)
XLA Ops:
  7.2 2.4 copy.37
  9.7 0.7 copy.32
  10.4 15.2 %all-to-all-start = ((s32[1,16,1]{2,0,1:T(1,128)}), s32[1,16,1]{2,0,1:T(1,128)S(1)}, u32[]{:S(2)}, u32[]{:S(2)}) async-start(s32[1,16,1]{2,0,1:T(1,128)} %copy.32), calls=%async_computation | async-start | bytes 16384 | tf_op jit(solution)/shard_map/all_to_all | solution.py:52
  25.6 1.7 copy.33
  27.3 2.1 copy.34
  29.4 0.9 gather_fusion
  30.3 1.8 fusion.8
  32.1 5.8 %all-to-all-done = s32[1,16,1]{2,0,1:T(1,128)S(1)} async-done(((s32[1,16,1]{2,0,1:T(1,128)}), s32[1,16,1]{2,0,1:T(1,128)S(1)}, u32[]{:S(2)}, u32[]{:S(2)}) %all-to-all-start) | async-done | bytes 96 | tf_op jit(solution)/shard_map/all_to_all | solution.py:52
  38.0 6.3 %all-to-all-start.1 = ((bf16[384,16,128]{2,0,1:T(8,128)(2,1)}), bf16[384,16,128]{2,0,1:T(8,128)(2,1)S(1)}, u32[]{:S(2)}, u32[]{:S(2)}) async-start(bf16[384,16,128]{2,0,1:T(8,128)(2,1)} %fusion.8), calls=%async_computation.1 | async-start | bytes 3145728 | tf_op jit(solution)/shard_map/all_to_all | solution.py:51
  44.4 186.3 %all-gather.3.cloned.1.call-done = bf16[1,384,16384]{1,2,0:T(8,128)(2,1)} async-done(((bf16[1,384,1024]{1,2,0:T(8,128)(2,1)}), bf16[1,384,16384]{1,2,0:T(8,128)(2,1)}) %all-gather.3.cloned.1.call-update) | async-done | bytes 12582928 | tf_op jit(solution)/shard_map/all_gather | solution.py:35
  230.7 15.8 %copy.38 = bf16[384,128,128]{2,0,1:T(8,128)(2,1)} copy(bf16[384,128,128]{0,2,1:T(8,128)(2,1)} %bitcast.64) | data formatting | bytes 25165824 | tf_op jit(solution)/shard_map/reshape | solution.py:37
  246.5 6.6 %gather_fusion.2 = bf16[16,384,128]{2,1,0:T(8,128)(2,1)} fusion(bf16[384,128,128]{2,0,1:T(8,128)(2,1)} %copy.38, s32[1024]{0:T(1024)S(1)} %pad_clamp_fusion), kind=kCustom, calls=%fused_computation.2 | custom fusion | bytes 3145792 | tf_op jit(solution)/shard_map/jit(_take)/gather | solution.py:36
  253.1 4.1 %broadcast_select_fusion.3 = (f32[16,128,128]{2,1,0:T(8,128)}, f32[1,1,16,128,128]{4,3,2,1,0:T(8,128)}) fusion(pred[16]{0:T(512)(128)(4,1)S(1)} %compare_bitcast_fusion, f32[1,1,16,128,128]{4,3,2,1,0:T(8,128)S(1)} %copy-done.3, bf16[16,384,128]{2,1,0:T(8,128)(2,1)} %copy-done.1, pred[16]{0:T(512)(128)(4,1)S(1)} %compare_and_fusion.1, ...), kind=kOutput, calls=%fused_computation.21 | convolution fusion | flops 203948032 | bytes 6291504 | tf_op jit(solution)/shard_map/tkc,tkf->kcf/dot_general | solution.py:39
  257.2 0.4 reduce
  257.6 0.9 fusion.24
  258.6 1.9 collective-permute-start.1
  260.5 2.4 collective-permute-start.2
  262.9 1.9 collective-permute-start
  264.9 1.4 collective-permute-done
  266.2 0.6 iota_compare_fusion.1
  266.9 0.2 copy.36
  267.1 0.7 gather_fusion.1
  267.8 0.8 bitcast_select_fusion
  268.6 74.6 %reduce-scatter.4.cloned.1.call-done = f32[1,128,128]{2,1,0:T(8,128)} async-done(((f32[16,128,128]{2,1,0:T(8,128)}), f32[1,128,128]{2,1,0:T(8,128)}) %reduce-scatter.4.cloned.1.call-update) | async-done | bytes 65552
  (32 shorter events, 0.2 us)
Async XLA Ops:
  7.2 23.1 %copy-start = (bf16[1,16,128,128]{3,2,1,0:T(8,128)(2,1)S(1)}, bf16[1,16,128,128]{3,2,1,0:T(8,128)(2,1)}, u32[]{:S(2)}) copy-start(bf16[1,16,128,128]{3,2,1,0:T(8,128)(2,1)} %param.11) | copy-start | bytes 1572868
  7.2 2.5 copy-start.5
  7.2 18.4 %copy-start.2 = (bf16[1,384,1664]{2,1,0:T(8,128)(2,1)S(1)}, bf16[1,384,1664]{2,1,0:T(8,128)(2,1)}, u32[]{:S(2)}) copy-start(bf16[1,384,1664]{2,1,0:T(8,128)(2,1)} %param.10) | copy-start | bytes 3833860
  7.2 223.5 %all-gather.3.cloned.1.call-start = ((), (), s32[]{:S(2)}) async-start(), calls=%async_computation.3 | async-start | bytes 13369344 | tf_op jit(solution)/shard_map/all_gather | solution.py:35
  10.4 27.6 %all-to-all-start = ((s32[1,16,1]{2,0,1:T(1,128)}), s32[1,16,1]{2,0,1:T(1,128)S(1)}, u32[]{:S(2)}, u32[]{:S(2)}) async-start(s32[1,16,1]{2,0,1:T(1,128)} %copy.32), calls=%async_computation | async-start | bytes 16384 | tf_op jit(solution)/shard_map/all_to_all | solution.py:52
  27.3 2.1 copy-start.4
  30.3 1.9 copy-start.1
  32.1 12.3 %copy-start.6 = (s32[1,1,16]{2,1,0:T(1,128)S(1)}, s32[1,1,16]{2,1,0:T(1,128)}, u32[]{:S(2)}) copy-start(s32[1,1,16]{2,1,0:T(1,128)} %param.15) | copy-start | bytes 196
  38.0 219.7 %all-to-all-start.1 = ((bf16[384,16,128]{2,0,1:T(8,128)(2,1)}), bf16[384,16,128]{2,0,1:T(8,128)(2,1)S(1)}, u32[]{:S(2)}, u32[]{:S(2)}) async-start(bf16[384,16,128]{2,0,1:T(8,128)(2,1)} %fusion.8), calls=%async_computation.1 | async-start | bytes 3145728 | tf_op jit(solution)/shard_map/all_to_all | solution.py:51
  44.3 298.9 %reduce-scatter.4.cloned.1.call-start = ((), (), s32[]{:S(2)}) async-start(), calls=%async_computation.4 | async-start | bytes 1114112
  246.5 6.6 %copy-start.3 = (f32[1,1,16,128,128]{4,3,2,1,0:T(8,128)S(1)}, f32[1,1,16,128,128]{4,3,2,1,0:T(8,128)}, u32[]{:S(2)}) copy-start(f32[1,1,16,128,128]{4,3,2,1,0:T(8,128)} %param.14) | copy-start | bytes 3145732
  257.2 3.3 copy-start.7
  258.6 8.3 %collective-permute-start.1 = (bf16[384,8,128]{2,1,0:T(8,128)(2,1)S(1)}, bf16[384,8,128]{2,1,0:T(8,128)(2,1)S(1)}, u32[]{:S(2)}, u32[]{:S(2)}) collective-permute-start(bf16[384,8,128]{2,1,0:T(8,128)(2,1)S(1)} %fusion.24), channel_id=1, source_target_pairs={{0,256},{256,0},{1,257},{257,1},{2,258},{258,2},{3,259},{259,3},{4... | collective-permute-start | bytes 2359304 | tf_op jit(solution)/shard_map/ppermute | solution.py:9
  260.5 6.3 %collective-permute-start.2 = (s32[12]{0:T(128)S(1)}, s32[12]{0:T(128)S(1)}, u32[]{:S(2)}, u32[]{:S(2)}) collective-permute-start(s32[12]{0:T(128)S(1)} %bitcast.68), channel_id=1, source_target_pairs={{0,256},{256,0},{1,257},{257,1},{2,258},{258,2},{3,259},{259,3},{4... | collective-permute-start | bytes 152 | tf_op jit(solution)/shard_map/ppermute | solution.py:9
  262.9 3.3 collective-permute-start
Sparse Core Ops, SparseCore 0:
  10.7 219.9 all-gather.2
  257.4 85.7 reduce-scatter.3
where the time goes:
time: 351 us; the launch traced here: 350 us
  waiting for transfers between devices  268 us (76%)
  local copies, waits for them, and re-layouts  31 us (9%)
  starting transfers between devices  27.9 us (8%)
  between operations  14.3 us (4%)
  matrix products  6.86 us (2%)
    all_gather x1, waiting for transfers between devices, local(): gathered = lax.all_gather(inputs, 'tensor', axis=1, tiled=True)  186 us
    unnamed x3, waiting for transfers between devices  74.6 us
    reshape x1, local copies, waits for them, and re-layouts, local(): gathered.reshape(tok_count, local_blocks * tensor_count, tile_size)  15.8 us
    all_to_all x1, starting transfers between devices, local(): lax.all_to_all(local_rows[None, :], 'tensor', split_axis=1, concat_axis=1...  15.2 us
  transfers between devices with their start and end apart: 7, of which 4 were waited for; matrix products, arithmetic and copies ran while one was open for 11% of the time, Pallas kernels for 0%

commit v1 on v0

--- a/solution.py
+++ b/solution.py
@@ -2,6 +2,7 @@
 import jax.numpy as jnp
 from jax import lax
 from jax.sharding import PartitionSpec as P
+from jax.lax import all_to_all, axis_size
 
 
 def shifted(value, axis, by):
@@ -32,7 +33,15 @@
     local_rows = row_ids % local_blocks
     grad_blocks = grads_out.reshape(tok_count, grads_out.shape[1] // tile_size, tile_size)
     grad_sel = jnp.take(grad_blocks, col_ids, axis=1)
-    gathered = lax.all_gather(inputs, "tensor", axis=1, tiled=True)
+    gathered = jnp.concatenate(
+        all_to_all(
+            jnp.stack(axis_size("tensor") * [inputs]),
+            axis_name="tensor",
+            split_axis=0,
+            concat_axis=0,
+        ),
+        axis=1,
+    )
     input_sel = jnp.take(
         gathered.reshape(tok_count, local_blocks * tensor_count, tile_size), row_ids, axis=1
     )

time: 351 us -> 722 us (2.06)
  waiting for transfers between devices: 268 us -> 624 us
  starting transfers between devices: 27.9 us -> 37.2 us
    all_to_all x0 -> x1, waiting for transfers between devices: none -> 534 us  [local(): all_to_all(jnp.stack(axis_size('tensor') * [inputs]), axis_name='tensor',...]
    all_gather x1 -> x0, waiting for transfers between devices: 186 us -> none  [local(): gathered = lax.all_gather(inputs, 'tensor', axis=1, tiled=True)]
    all_to_all x1, waiting for transfers between devices: 0.01 us -> 47.3 us  [local(): lax.all_to_all(partial_value, 'tensor', split_axis=1, concat_axis=1, tile...]
    unnamed x3 -> x2, waiting for transfers between devices: 74.6 us -> 30.9 us
    another operation x0 -> x3, local copies, waits for them, and re-layouts: none -> 23.3 us  [the longest x1 15.7 us: local(): gathered.reshape(tok_count, local_blocks * tensor_count, tile_size)]
    reshape x1 -> x0, local copies, waits for them, and re-layouts: 15.8 us -> none  [local(): gathered.reshape(tok_count, local_blocks * tensor_count, tile_size)]
  transfers between devices with their start and end apart: 7 -> 7, of which waited for: 4 -> 5; matrix products, arithmetic and copies ran while one was open for 11% -> 5% of each run, Pallas kernels for 0% -> 0%
where the time goes in v1:
time: 722 us; the launch traced here: 721 us
  waiting for transfers between devices  624 us (86%)
  starting transfers between devices  37.2 us (5%)
  local copies, waits for them, and re-layouts  36.1 us (5%)
  between operations  14.3 us (2%)
    all_to_all x1, waiting for transfers between devices, local(): all_to_all(jnp.stack(axis_size('tensor') * [inputs]), axis_name='tensor',...  534 us
    all_to_all x1, waiting for transfers between devices, local(): lax.all_to_all(partial_value, 'tensor', split_axis=1, concat_axis=1, tile...  47.3 us
    unnamed x2, waiting for transfers between devices  30.9 us
    another operation x1, local copies, waits for them, and re-layouts, local(): gathered.reshape(tok_count, local_blocks * tensor_count, tile_size)  15.7 us
    all_to_all x1, starting transfers between devices, local(): lax.all_to_all(local_rows[None, :], 'tensor', split_axis=1, concat_axis=1...  15.2 us
  transfers between devices with their start and end apart: 7, of which 5 were waited for; matrix products, arithmetic and copies ran while one was open for 5% of the time, Pallas kernels for 0%

profile of v1, /device:TPU:2, one launch (start us, length us, event | category | flops | bytes accessed | tf_op | source)
XLA Modules:
  0.0 721.4 jit_solution(13819748071034006781)
XLA Ops:
  7.2 0.7 fusion.32
  7.9 0.7 copy.27
  8.6 15.2 %all-to-all-start = ((s32[1,16,1]{2,0,1:T(1,128)}), s32[1,16,1]{2,0,1:T(1,128)S(1)}, u32[]{:S(2)}, u32[]{:S(2)}) async-start(s32[1,16,1]{2,0,1:T(1,128)} %copy.27), calls=%async_computation | async-start | bytes 16384 | tf_op jit(solution)/shard_map/all_to_all | solution.py:61
  23.8 1.5 copy.32
  25.3 10.9 %all-to-all-done = s32[1,16,1]{2,0,1:T(1,128)S(1)} async-done(((s32[1,16,1]{2,0,1:T(1,128)}), s32[1,16,1]{2,0,1:T(1,128)S(1)}, u32[]{:S(2)}, u32[]{:S(2)}) %all-to-all-start) | async-done | bytes 96 | tf_op jit(solution)/shard_map/all_to_all | solution.py:61
  36.1 6.1 stack.3
  42.2 5.1 all-to-all-start.2
  47.3 1.7 copy.28
  49.1 2.1 copy.29
  51.2 0.9 gather_fusion
  52.1 1.8 fusion.8
  53.9 534.1 %all-to-all-done.2 = bf16[16,384,1024]{1,2,0:T(8,128)(2,1)} async-done(((bf16[16,384,1024]{1,2,0:T(8,128)(2,1)}), bf16[16,384,1024]{1,2,0:T(8,128)(2,1)}, u32[]{:S(2)}, u32[]{:S(2)}) %all-to-all-start.2) | async-done | bytes 12582944 | tf_op jit(solution)/shard_map/all_to_all | solution.py:37
  588.0 10.6 %all-to-all-start.1 = ((bf16[384,16,128]{2,0,1:T(8,128)(2,1)}), bf16[384,16,128]{2,0,1:T(8,128)(2,1)S(1)}, u32[]{:S(2)}, u32[]{:S(2)}) async-start(bf16[384,16,128]{2,0,1:T(8,128)(2,1)} %fusion.8), calls=%async_computation.1 | async-start | bytes 3145728 | tf_op jit(solution)/shard_map/all_to_all | solution.py:60
  598.7 15.7 %copy.33 = bf16[384,128,128]{2,0,1:T(8,128)(2,1)} copy(bf16[384,128,128]{0,2,1:T(8,128)(2,1)} %bitcast.18) | data formatting | bytes 25165824 | tf_op jit(solution)/shard_map/reshape;reshape | solution.py:46
  614.5 6.6 gather_fusion.2
  621.0 4.1 broadcast_select_fusion.3
  625.5 47.3 %all-to-all-done.1 = bf16[384,16,128]{2,0,1:T(8,128)(2,1)S(1)} async-done(((bf16[384,16,128]{2,0,1:T(8,128)(2,1)}), bf16[384,16,128]{2,0,1:T(8,128)(2,1)S(1)}, u32[]{:S(2)}, u32[]{:S(2)}) %all-to-all-start.1) | async-done | bytes 1572896 | tf_op jit(solution)/shard_map/all_to_all | solution.py:60
  672.9 0.9 fusion.24
  673.8 1.9 collective-permute-start.1
  675.8 2.4 collective-permute-start.2
  678.2 1.9 collective-permute-start
  680.1 1.2 collective-permute-done
  682.8 0.8 bitcast_select_fusion
  683.7 30.9 %reduce-scatter.4.cloned.1.call-done = f32[1,128,128]{2,1,0:T(8,128)} async-done(((f32[16,128,128]{2,1,0:T(8,128)}), f32[1,128,128]{2,1,0:T(8,128)}) %reduce-scatter.4.cloned.1.call-update) | async-done | bytes 65552
  (32 shorter events, 2.0 us)
Async XLA Ops:
  7.2 44.9 %copy-start = (bf16[1,16,128,128]{3,2,1,0:T(8,128)(2,1)S(1)}, bf16[1,16,128,128]{3,2,1,0:T(8,128)(2,1)}, u32[]{:S(2)}) copy-start(bf16[1,16,128,128]{3,2,1,0:T(8,128)(2,1)} %param.11) | copy-start | bytes 1572868
  8.6 27.6 %all-to-all-start = ((s32[1,16,1]{2,0,1:T(1,128)}), s32[1,16,1]{2,0,1:T(1,128)S(1)}, u32[]{:S(2)}, u32[]{:S(2)}) async-start(s32[1,16,1]{2,0,1:T(1,128)} %copy.27), calls=%async_computation | async-start | bytes 16384 | tf_op jit(solution)/shard_map/all_to_all | solution.py:61
  42.2 5.1 copy-start.2
  42.2 545.7 %all-to-all-start.2 = ((bf16[16,384,1024]{1,2,0:T(8,128)(2,1)}), bf16[16,384,1024]{1,2,0:T(8,128)(2,1)}, u32[]{:S(2)}, u32[]{:S(2)}) async-start(bf16[16,384,1024]{1,2,0:T(8,128)(2,1)} %stack.3), calls=%async_computation.2 | async-start | bytes 25165824 | tf_op jit(solution)/shard_map/all_to_all | solution.py:37
  49.0 2.1 copy-start.4
  52.0 1.9 copy-start.1
  53.9 544.8 %copy-start.5 = (s32[1,16]{1,0:T(1,128)S(1)}, s32[1,16]{1,0:T(1,128)}, u32[]{:S(2)}) copy-start(s32[1,16]{1,0:T(1,128)} %param.12) | copy-start | bytes 196
  53.9 544.8 %copy-start.6 = (s32[1,1,16]{2,1,0:T(1,128)S(1)}, s32[1,1,16]{2,1,0:T(1,128)}, u32[]{:S(2)}) copy-start(s32[1,1,16]{2,1,0:T(1,128)} %param.15) | copy-start | bytes 196
  588.0 84.9 %all-to-all-start.1 = ((bf16[384,16,128]{2,0,1:T(8,128)(2,1)}), bf16[384,16,128]{2,0,1:T(8,128)(2,1)S(1)}, u32[]{:S(2)}, u32[]{:S(2)}) async-start(bf16[384,16,128]{2,0,1:T(8,128)(2,1)} %fusion.8), calls=%async_computation.1 | async-start | bytes 3145728 | tf_op jit(solution)/shard_map/all_to_all | solution.py:60
  598.6 116.0 %reduce-scatter.4.cloned.1.call-start = ((), (), s32[]{:S(2)}) async-start(), calls=%async_computation.4 | async-start | bytes 1114112
  614.5 6.6 copy-start.3
  625.1 50.6 %copy-start.7 = (s32[1,1,12]{2,1,0:T(1,128)S(1)}, s32[1,1,12]{2,1,0:T(1,128)}, u32[]{:S(2)}) copy-start(s32[1,1,12]{2,1,0:T(1,128)} %param.16) | copy-start | bytes 148
  673.8 8.1 %collective-permute-start.1 = (bf16[384,8,128]{2,1,0:T(8,128)(2,1)S(1)}, bf16[384,8,128]{2,1,0:T(8,128)(2,1)S(1)}, u32[]{:S(2)}, u32[]{:S(2)}) collective-permute-start(bf16[384,8,128]{2,1,0:T(8,128)(2,1)S(1)} %fusion.24), channel_id=1, source_target_pairs={{0,256},{256,0},{1,257},{257,1},{2,258},{258,2},{3,259},{259,3},{4... | collective-permute-start | bytes 2359304 | tf_op jit(solution)/shard_map/ppermute | solution.py:10
  675.8 6.2 collective-permute-start.2
  678.2 3.1 collective-permute-start
Sparse Core Ops, SparseCore 0:
  625.3 89.2 reduce-scatter.3
